TPU v7x, 512 devices: a whole 4x8x8 slice. The times are simulated.
512 devices in a mesh: dp: 8 (over z), fsdp: 64 (over y, x, core).
Axes of the slice: x: 4, y: 8, z: 8, core: 2. Of those that a mesh axis runs over, the one named last changes fastest.
Arguments:
- gradients: bfloat16 [8, 512, 512, 512], P('dp', 'fsdp'), may hold values from -48 to 48
- owners: int32 [8, 64], P('dp'), may hold values from 0 to 63, as said below
Outputs:
- updates: bfloat16 [512, 512, 512], P('fsdp', 'dp')
- owner_scales: float32 [8, 64, 2], P('dp', 'fsdp')
Inputs may be any that keep to these rules, and one draw needn't show every extreme that they name: Each entry names the owner of that block among the fsdp indices; no owner holds more than 2 blocks of a group, and in every group some owners hold exactly 2.
All inputs are finite; a program needn't handle non-finite values.
Results may differ from a plain program's by a relative error of at most 0.02.
Values may be sent and summed in bfloat16 or wider, within the bound.
A program may use at most 64 MiB of HBM per device.

v0:
```python
import jax
import jax.numpy as jnp
from jax import lax
from jax.sharding import PartitionSpec as P

MOST = 2


def product(left_side, right_side):
    return jnp.dot(left_side, right_side, preferred_element_type=jnp.float32)


def inverse_root(factor):
    identity = jnp.eye(factor.shape[0], dtype=jnp.float32)
    factor_norm = jnp.sqrt(jnp.sum(factor * factor) + 1e-06)
    scaled = factor / factor_norm
    scaled_low = scaled.astype(jnp.bfloat16)
    first_step = ((5.0 * identity - scaled) * 0.25).astype(jnp.bfloat16)
    step_square = product(first_step, first_step).astype(jnp.bfloat16)
    partial_term = product(step_square, scaled_low).astype(jnp.bfloat16)
    next_scaled = product(step_square, partial_term)
    second_step = ((5.0 * identity - next_scaled) * 0.25).astype(jnp.bfloat16)
    return product(first_step, second_step).astype(jnp.bfloat16)


def precondition_low(block_low, grad_squares):
    left_factor = product(block_low, block_low.T)
    right_factor = product(block_low.T, block_low)
    root_left = inverse_root(left_factor)
    root_right = inverse_root(right_factor)
    half_applied = product(root_left, block_low).astype(jnp.bfloat16)
    direction = product(half_applied, root_right)
    grad_norm = jnp.sqrt(grad_squares)
    direction_norm = jnp.sqrt(jnp.sum(direction * direction) + 1e-06)
    graft_scale = grad_norm / direction_norm
    return ((graft_scale * direction).astype(jnp.bfloat16), graft_scale)


def slot_selector(owner_rows, owner_count):
    devices = jnp.arange(owner_count, dtype=jnp.int32)
    owned_by = (owner_rows[..., :, None] == devices).astype(jnp.int32)
    earlier = jnp.cumsum(owned_by, axis=-2) - owned_by
    slot_index = jnp.sum(earlier * owned_by, axis=-1)
    slots = jnp.arange(MOST, dtype=jnp.int32)
    selector = (owner_rows[..., None, None, :] == devices[:, None, None]) & (
        slot_index[..., None, None, :] == slots[None, :, None]
    )
    return selector.astype(jnp.float32)


def on_device(gradients, owners):
    summed = lax.psum_scatter(
        gradients[0].astype(jnp.float32).astype(jnp.bfloat16), "dp", scatter_dimension=1, tiled=True
    ).astype(jnp.float32)
    fsdp_count = lax.axis_size("fsdp")
    my_index = lax.axis_index("fsdp")
    selector = slot_selector(owners[0], fsdp_count)
    arrived = lax.all_to_all(summed, "fsdp", split_axis=1, concat_axis=0, tiled=True)
    whole_block = arrived[:, 0, :]
    block_update, block_scale = precondition_low(
        whole_block.astype(jnp.bfloat16), jnp.sum(whole_block * whole_block)
    )
    update_out = lax.all_to_all(
        block_update[:, None, :], "fsdp", split_axis=0, concat_axis=1, tiled=True
    )
    group_scales = lax.all_gather(block_scale.reshape(1), "fsdp", axis=0, tiled=True)
    my_slots = lax.dynamic_index_in_dim(selector, my_index, 0, keepdims=False)
    owner_scales = jnp.sum(my_slots * group_scales[None, :], axis=1)
    return (update_out, owner_scales.reshape(1, 1, MOST))


def solution(mesh):
    placed = (P("dp", "fsdp", None, None), P("dp", None))
    return jax.shard_map(
        on_device,
        mesh=mesh,
        in_specs=placed,
        out_specs=(P("fsdp", "dp", None), P("dp", "fsdp", None)),
        check_vma=False,
    )
```

profile of v0, /device:TPU:1, one launch (start us, length us, event | category | flops | bytes accessed | tf_op | source)
XLA Modules:
  0.0 287.3 jit_solution(1662580952846874514)
XLA Ops:
  7.2 6.5 %copy.41 = bf16[1,8,512,512]{3,1,2,0:T(8,128)(2,1)} copy(bf16[1,8,512,512]{3,2,1,0:T(8,128)(2,1)} %param.2) | data formatting | bytes 8388608 | tf_op args[0]
  13.7 64.4 %reduce-scatter.2.cloned.1.call-done = bf16[8,64,512]{2,0,1:T(8,128)(2,1)} async-done(((bf16[8,512,512]{2,0,1:T(8,128)(2,1)}), bf16[8,64,512]{2,0,1:T(8,128)(2,1)}) %reduce-scatter.2.cloned.1.call-update) | async-done | bytes 524304 | tf_op jit(solution)/shard_map/reduce_scatter | solution.py:52
  78.1 1.2 convert_element_type.73
  79.3 38.1 %all_to_all.27 = f32[8,64,512]{2,0,1:T(8,128)S(1)} all-to-all(f32[8,64,512]{2,0,1:T(8,128)S(1)} %convert_element_type.73), channel_id=1, replica_groups=mesh['dp'=8,'fsdp'=64] {'fsdp'}, dimensions={1} | all-to-all | bytes 2097152 | tf_op jit(solution)/shard_map/all_to_all | solution.py:58
  117.4 0.6 copy.43
  118.0 1.5 multiply_reduce_fusion.2
  120.1 0.2 fusion.6
  120.3 0.4 convolution_convert_fusion.6
  120.7 0.8 copy-done
  121.5 1.3 convolution_convert_fusion.5
  122.8 2.8 convolution_convert_fusion.4
  125.5 2.0 multiply_reduce_fusion.1
  128.2 0.2 fusion.8
  128.4 0.4 convolution_convert_fusion.2
  128.9 0.8 copy-done.1
  129.6 1.3 convolution_convert_fusion.1
  130.9 2.8 convolution_convert_fusion
  133.7 2.8 multiply_reduce_fusion
  137.2 0.9 multiply_reduce_fusion.3
  138.8 0.1 fusion.9
  138.9 0.5 broadcast.80
  139.4 1.0 reduce.3
  140.4 1.0 reshape.82
  141.4 6.5 %all-to-all-start.1 = ((bf16[64,2,2048]{2,1,0:T(2,128)(2,1)}), bf16[64,2,2048]{2,1,0:T(2,128)(2,1)S(1)}, u32[]{:S(2)}, u32[]{:S(2)}) async-start(bf16[64,2,2048]{2,1,0:T(2,128)(2,1)} %reshape.82), calls=%async_computation.2 | async-start | bytes 1048576 | tf_op jit(solution)/shard_map/all_to_all | solution.py:63
  148.1 1.3 dynamic-slice
  149.5 0.2 select_reduce_fusion
  149.7 0.8 dynamic-update-slice
  150.5 127.8 %all-reduce = f32[64]{0:T(128)S(1)} all-reduce(f32[64]{0:T(128)S(1)} %dynamic-update-slice), channel_id=1, replica_groups=mesh['dp'=8,'fsdp'=64] {'fsdp'}, use_global_device_ids=true, to_apply=%add | all-reduce | flops 64 | bytes 512
  278.2 0.6 fusion.30
  278.9 0.5 reshape.83
  279.4 0.1 copy.42
  279.5 0.9 copy.16
  (12 shorter events, 0.3 us)
Async XLA Ops:
  7.2 70.9 %reduce-scatter.2.cloned.1.call-start = ((), (), s32[]{:S(2)}) async-start(), calls=%async_computation.3 | async-start | bytes 4718592 | tf_op jit(solution)/shard_map/reduce_scatter | solution.py:52
  120.7 0.8 copy-start
  128.8 0.8 copy-start.1
  133.7 14.2 %copy-start.2 = (s32[1,64]{1,0:T(1,128)S(1)}, s32[1,64]{1,0:T(1,128)}, u32[]{:S(2)}) copy-start(s32[1,64]{1,0:T(1,128)} %param.3) | copy-start | bytes 772
  141.4 137.4 %all-to-all-start.1 = ((bf16[64,2,2048]{2,1,0:T(2,128)(2,1)}), bf16[64,2,2048]{2,1,0:T(2,128)(2,1)S(1)}, u32[]{:S(2)}, u32[]{:S(2)}) async-start(bf16[64,2,2048]{2,1,0:T(2,128)(2,1)} %reshape.82), calls=%async_computation.2 | async-start | bytes 1048576 | tf_op jit(solution)/shard_map/all_to_all | solution.py:63
Sparse Core Ops, SparseCore 0:
  13.8 64.2 reduce-scatter.1
where the time goes:
time: 290 us; the launch traced here: 287 us
  blocking collectives  166 us (57%)
  waiting for transfers between devices  64.4 us (22%)
  between operations  16.9 us (6%)
  matrix products  15.2 us (5%)
  local copies, waits for them, and re-layouts  13.9 us (5%)
  starting transfers between devices  6.51 us (2%)
  other arithmetic  4.46 us (2%)
    unnamed x1, blocking collectives  128 us
    reduce_scatter x1, waiting for transfers between devices, on_device(): lax.psum_scatter(gradients[0].astype(jnp.float32).astype(jnp.bfloat16), '...  64.4 us
    all_to_all x1, blocking collectives, on_device(): lax.all_to_all(summed, 'fsdp', split_axis=1, concat_axis=0, tiled=True)  38.1 us
    dot_general x9, matrix products, product(): return jnp.dot(left_side, right_side, preferred_element_type=jnp.float32)  15.2 us
    unnamed x14, local copies, waits for them, and re-layouts  12.8 us
    all_to_all x1, starting transfers between devices, on_device(): lax.all_to_all(block_update[:, None, :], 'fsdp', split_axis=0, concat_axi...  6.47 us
  transfers between devices with their start and end apart: 2, of which 1 were waited for; matrix products, arithmetic and copies ran while one was open for 1% of the time, Pallas kernels for 0%

commit v1 on v0

v1 whole, which is shorter than its diff:
```python
import functools

import jax
import jax.numpy as jnp
from jax import lax
from jax.experimental import pallas as pl
from jax.experimental.pallas import tpu as pltpu
from jax.sharding import PartitionSpec as P

MOST = 2
PARTS = 4
SUBS = 2 * PARTS
SLOTS = 4
STARTS = (8, 12, 12, 12)
PERIODS = 16
LANE = 128
LINES = 8
FAR_FIRST = (4, -3, 3, -2, 2, -1, 1, 0)
ACROSS = 4
CORES = 2
MESH = pl.DeviceIdType.MESH


def product(left_side, right_side):
    return jnp.dot(left_side, right_side, preferred_element_type=jnp.float32)


def fives(size):
    shape = (size, size)
    down = lax.broadcasted_iota(jnp.int32, shape, 0)
    across = lax.broadcasted_iota(jnp.int32, shape, 1)
    return jnp.where(down == across, 5.0, 0.0)


def within(index, count):
    return jnp.where(index >= count, index - count, index)


def wave_of(device):
    core = lax.rem(device, CORES)
    chip = lax.div(device, CORES)
    column, row = lax.rem(chip, ACROSS), lax.div(chip, ACROSS)
    return CORES * core + lax.rem(column + row, 2), row * (ACROSS // 2) + lax.div(column, 2)


def each_receiver(part, device, batch, send):
    core, parity = lax.div(part, CORES), lax.rem(part, CORES)
    chip = lax.div(device, CORES)
    first, mine = lax.div(lax.rem(chip, ACROSS), 2), lax.div(chip, ACROSS)
    even = lax.rem(parity + mine, 2)
    for offset in FAR_FIRST[2 * batch : 2 * batch + 2]:
        row = within(mine + offset % LINES, LINES)
        odd = 1 - even if offset % 2 else even
        for pair in (first, 1 - first):
            column = 2 * pair + odd
            send(row * (ACROSS // 2) + pair, (row * ACROSS + column) * CORES + core)


def blocks_stepped(index):
    lane, row = index >> 3, index & 7
    core, column = lane & 1, lane >> 1
    wave = 2 * core + ((column + row) & 1)
    return wave * 16 + row * 2 + (column >> 1)


def step_kernel(
    planes, count, x_ref, owners_ref, out_ref, slots_ref,
    own, come, turned, ready, gathered, back, returned, scale_mine, column_scales, scales, restored,
    block, scaled_low, first_step, step_square, partial_term, second_step, root, half_applied,
    grad_squares,
    load_sem, send_sem, recv_sem, push_sem, block_sem, row_sem, column_sem, scale_sem, plane_sem,
):
    plane = lax.axis_index("dp")
    me = lax.axis_index("fsdp")
    half = planes // 2
    group = count
    part_size = group // PARTS
    rows, width = out_ref.shape[0], out_ref.shape[2] // 2
    few = rows // 2
    lanes = ACROSS * CORES
    lines = count // lanes
    my_line, my_lane = lax.div(me, lanes), lax.rem(me, lanes)
    my_wave, my_place = wave_of(me)
    my_block = my_wave * part_size + my_place
    barrier = pltpu.get_barrier_semaphore()

    goals = [
        [within(plane + (far if way == 0 else planes - far), planes) for far in range(half + 1)]
        for way in (0, 1)
    ]

    def goal(way, far):
        return goals[way][far]

    def blocks(part):
        return pl.ds(pl.multiple_of(part * part_size, part_size), part_size)

    def place_of(sub):
        return pl.ds(lax.rem(sub, 2) * few, few), lax.div(sub, 2)

    def raw(way, far, sub):
        lines_of, part = place_of(sub)
        first = pl.multiple_of(goal(way, far) * group + part * part_size, part_size)
        return x_ref.at[0, lines_of, pl.ds(first, part_size), :]

    def slot(way, far):
        return 0 if far == 0 else far + way * (half - 1)

    def kept(way, far, sub):
        lines_of, part = place_of(sub)
        return own.at[slot(way, far), lines_of, blocks(part), :]

    def landed(way, far, sub):
        lines_of, part = place_of(sub)
        return come.at[way, far - 1, lines_of, blocks(part), :]

    def copy(way, far, sub, source):
        return pltpu.make_async_remote_copy(
            src_ref=source,
            dst_ref=landed(way, far, sub),
            send_sem=send_sem.at[way, far - 1, sub],
            recv_sem=recv_sem.at[way, far - 1, sub],
            device_id=(goal(way, 1), me),
            device_id_type=MESH,
        )

    def arrived(way, far, sub):
        copy(way, far, sub, landed(way, far, sub)).wait_recv()

    def load(way, far):
        first, size = (way * few, few) if far == half - 1 else (0, rows)
        start = pl.multiple_of(goal(way, far) * group, group)
        return pltpu.make_async_copy(
            x_ref.at[0, pl.ds(first, size), pl.ds(start, group), :],
            own.at[slot(way, far), pl.ds(first, size), :, :],
            load_sem.at[slot(way, far)],
        )

    def relay(way, far, sub):
        arrived(way, far + 1, sub)
        mine = kept(way, far, sub)
        total = mine[...].astype(jnp.float32) + landed(way, far + 1, sub)[...].astype(jnp.float32)
        mine[...] = total.astype(jnp.bfloat16)
        copy(way, far, sub, mine).start()

    def first_relay(sub):
        far = half - 1
        for way in (0, 1):

            @pl.when(lax.rem(sub, 2) != way)
            def _():
                copy(way, far, sub, raw(way, far, sub)).start()
                relay(1 - way, far, sub)

    def push(source, target, other, sent, got):
        pltpu.make_async_remote_copy(
            src_ref=source,
            dst_ref=target,
            send_sem=sent,
            recv_sem=got,
            device_id=(plane, other),
            device_id_type=MESH,
        ).start()

    def settle(buffer, semaphore):
        pltpu.make_async_copy(buffer, buffer, semaphore).wait()

    def in_column(step):
        return within(me + step * lanes, count)

    def in_row(step):
        return my_line * lanes + within(my_lane + step, lanes)

    def finish(sub):
        arrived(0, 1, sub)
        arrived(1, 1, sub)
        total = kept(0, 0, sub)[...].astype(jnp.float32)
        total += landed(0, 1, sub)[...].astype(jnp.float32)
        total += landed(1, 1, sub)[...].astype(jnp.float32)
        flat = total.reshape(few * part_size, 2 * width)
        tiles = [turned.at[tile] for tile in range(2 * width // LANE)]
        start = pl.multiple_of(lax.rem(sub, 2) * (few * part_size), few * part_size)
        for tile, lane in enumerate(tiles):
            lane[pl.ds(start, few * part_size), :] = flat[:, tile * LANE : (tile + 1) * LANE]

        @pl.when(lax.rem(sub, 2) == 1)
        def _():
            part = lax.div(sub, 2)
            for index in range(part_size):
                pieces = [lane[pl.ds(index, rows, stride=part_size), :] for lane in tiles]
                message = [
                    jnp.concatenate(pieces[: len(pieces) // 2], axis=1),
                    jnp.concatenate(pieces[len(pieces) // 2 :], axis=1),
                ]
                ready[part * part_size + index] = jnp.concatenate(message, axis=0).astype(
                    jnp.bfloat16
                )

    def hand_out(part, batch):
        def send(place, other):
            source = ready.at[part * part_size + place]

            @pl.when(other != me)
            def _():
                push(source, gathered.at[me], other, push_sem.at[0], block_sem)

            @pl.when(other == me)
            def _():
                pltpu.make_async_copy(source, gathered.at[me], block_sem).start()

        each_receiver(part, me, batch, send)

    size = count * rows

    def take_block():
        settle(gathered, block_sem)
        received = gathered[...].astype(jnp.float32)
        sides = [received[:, :rows, :], received[:, rows:, :]]
        whole = jnp.concatenate([side.reshape(size, width) for side in sides], axis=1)
        grad_squares[...] = jnp.broadcast_to(
            jnp.sum(whole * whole, keepdims=True), grad_squares.shape
        )
        block[...] = whole.astype(jnp.bfloat16)

    def take_factor():
        factor = lax.dot_general(
            block[...], block[...], (((1,), (1,)), ((), ())), preferred_element_type=jnp.float32
        )
        scaled = factor * (1.0 / jnp.sqrt(jnp.sum(factor * factor, keepdims=True) + 1e-06))
        scaled_low[...] = scaled.astype(jnp.bfloat16)
        first_step[...] = ((fives(size) - scaled) * 0.25).astype(jnp.bfloat16)

    def take_square():
        step_square[...] = product(first_step[...], first_step[...]).astype(jnp.bfloat16)

    def take_partial():
        partial_term[...] = product(step_square[...], scaled_low[...]).astype(jnp.bfloat16)

    def take_second():
        next_scaled = product(step_square[...], partial_term[...])
        second_step[...] = ((fives(size) - next_scaled) * 0.25).astype(jnp.bfloat16)

    def take_root():
        root[...] = product(first_step[...], second_step[...]).astype(jnp.bfloat16)

    def take_half():
        half_applied[...] = product(root[...], block[...]).astype(jnp.bfloat16)

    def take_direction():
        direction = product(root[...], half_applied[...])
        graft = jnp.sqrt(grad_squares[...][:, :1]) / jnp.sqrt(
            jnp.sum(direction * direction, keepdims=True) + 1e-06
        )
        update = direction * graft
        sides = [update[:, :width], update[:, width:]]
        back[...] = jnp.concatenate(
            [side.reshape(count, rows, width) for side in sides], axis=1
        ).astype(jnp.bfloat16)
        scale_mine[...] = jnp.broadcast_to(graft, scale_mine.shape)

    def give_scale():
        def line(step, carry):
            push(scale_mine, column_scales.at[my_line], in_column(step), push_sem.at[2], column_sem)
            return carry

        lax.fori_loop(1, lines, line, 0)
        pltpu.make_async_copy(scale_mine, column_scales.at[my_line], column_sem).start()
        pltpu.make_async_copy(back.at[me], returned.at[my_block], row_sem.at[my_wave]).start()

    def give_rows(quarter):
        def to_lane(step, carry):
            lane = within(my_lane + step, lanes)
            for offset in FAR_FIRST:
                other = within(my_line + offset % lines, lines) * lanes + lane

                @pl.when(other != me)
                def _():
                    push(
                        back.at[other], returned.at[my_block], other,
                        push_sem.at[1], row_sem.at[my_wave],
                    )

            return carry

        lax.fori_loop(quarter * lanes // 4, (quarter + 1) * lanes // 4, to_lane, 0)

    def first_rows():
        give_scale()
        give_rows(0)

    stages = [
        take_block, take_factor, take_square, take_partial, take_second, take_root, take_half,
        take_direction, first_rows, *[functools.partial(give_rows, q) for q in (1, 2, 3)],
    ]

    loads = [load(way, far) for far in range(half - 1, 0, -1) for way in (0, 1)] + [load(0, 0)]
    for each in loads:
        each.start()
    def signal(semaphore, device):
        pl.semaphore_signal(semaphore, inc=1, device_id=device, device_id_type=MESH)

    def greet_column(step, carry):
        signal(barrier, (plane, in_column(step)))
        return carry

    def greet_row(step, carry):
        signal(barrier, (plane, in_row(step)))
        return carry

    def vouch(step, carry):
        signal(plane_sem, (plane, in_row(step)))
        return carry

    signal(barrier, (goal(0, 1), me))
    signal(barrier, (goal(1, 1), me))
    lax.fori_loop(1, lines, greet_column, 0)
    lax.fori_loop(1, lanes, greet_row, 0)
    pl.semaphore_wait(barrier, lines + lanes)

    def start_half_way(pair, carry):
        for way in (0, 1):
            sub = 2 * pair + way
            copy(way, half, sub, raw(way, half, sub)).start()
        return carry

    lax.fori_loop(0, SUBS // 2, start_half_way, 0)
    lax.fori_loop(1, lanes, vouch, 0)
    for each in loads:
        each.wait()
    first_relay(0)
    pl.semaphore_wait(plane_sem, lanes - 1)
    begin = STARTS[-1]
    for wave in reversed(range(PARTS - 1)):
        begin = jnp.where(my_wave == wave, STARTS[wave], begin)

    def period(now, carry):
        for turn in range(SLOTS):
            far = SLOTS - 1 - turn
            if far < half:
                lag = 2 * (half - far) - 3 if far else 2 * (half - 2)
                sub = now - lag

                @pl.when((sub >= 0) & (sub < SUBS))
                def _():
                    if far == half - 1:
                        first_relay(sub)
                    elif far > 0:
                        relay(0, far, sub)
                        relay(1, far, sub)
                    else:
                        finish(sub)

            lag = 2 * (half - 2) + (0 if turn == SLOTS - 1 else 1)
            last = now - lag

            @pl.when((last >= 0) & (last < SUBS) & (lax.rem(last + SUBS, 2) == 1))
            def _():
                hand_out(lax.div(last, 2), (turn + 1) % SLOTS)

            for number, stage in enumerate(stages):
                if (number + SLOTS - 1) % SLOTS == turn:
                    pl.when(now == begin + (number + SLOTS - 1) // SLOTS)(stage)
        return carry

    lax.fori_loop(0, PERIODS, period, 0)

    settle(column_scales, column_sem)
    mine_there = scales.at[pl.ds(my_lane * lines, lines)]

    def spread(step, carry):
        push(column_scales, mine_there, in_row(step), push_sem.at[3], scale_sem)
        return carry

    lax.fori_loop(1, lanes, spread, 0)
    pltpu.make_async_copy(column_scales, mine_there, scale_sem).start()

    def sent(pair, carry):
        for way in (0, 1):
            copy(way, half, 2 * pair + way, landed(way, half, 2 * pair + way)).wait_send()
            for far in range(1, half):
                for sub in (2 * pair, 2 * pair + 1):
                    copy(way, far, sub, landed(way, far, sub)).wait_send()
        return carry

    lax.fori_loop(0, SUBS // 2, sent, 0)
    settle(ready.at[pl.ds(0, count - 1)], push_sem.at[0])
    def restore(part, carry):
        settle(returned.at[blocks(part)], row_sem.at[part])
        flat = returned[blocks(part)].astype(jnp.float32).reshape(part_size * 2 * rows, width)
        for tile in range(width // LANE):
            lane = restored.at[tile]
            lane[...] = flat[:, tile * LANE : (tile + 1) * LANE]
            for side in range(2):
                first = side * width + tile * LANE
                for row in range(rows):
                    column = lane[pl.ds(side * rows + row, part_size, stride=2 * rows), :]
                    out_ref[row, blocks(part), first : first + LANE] = column.astype(jnp.bfloat16)
        return carry

    lax.fori_loop(0, PARTS - 1, restore, 0)
    settle(scales, scale_sem)
    factors = scales[...][:, 0, :1]
    square = (count, count)
    mine = jnp.broadcast_to((owners_ref[...] == me).astype(jnp.float32), square)
    stepped = blocks_stepped(lax.broadcasted_iota(jnp.int32, square, 0))
    across = lax.broadcasted_iota(jnp.int32, square, 1)
    owned = jnp.sum(jnp.where(across == stepped, mine, 0.0), axis=1, keepdims=True)
    earlier = jnp.sum(jnp.where(across < stepped, mine, 0.0), axis=1, keepdims=True)
    place = lax.broadcasted_iota(jnp.int32, (count, MOST), 1).astype(jnp.float32)
    picked = jnp.where((earlier == place) & (owned > 0.5), factors, 0.0)
    slots_ref[0] = jnp.sum(picked, axis=0, keepdims=True)
    restore(PARTS - 1, 0)

    settle(back.at[pl.ds(0, count - 1)], push_sem.at[1])
    settle(column_scales.at[pl.ds(0, lines - 1)], push_sem.at[2])
    settle(scales.at[pl.ds(0, (lanes - 1) * lines)], push_sem.at[3])


def on_device(gradients, owners):
    planes, count = lax.axis_size("dp"), lax.axis_size("fsdp")
    _, rows, blocks, width = gradients.shape
    group = blocks // planes
    half = planes // 2
    part_size = group // PARTS
    lines = count // (ACROSS * CORES)
    message = (group, 2 * rows, width // 2)
    matrix = (count * rows, count * rows)
    vmem = pl.BlockSpec(memory_space=pltpu.VMEM)
    return pl.pallas_call(
        functools.partial(step_kernel, planes, count),
        out_shape=(
            jax.ShapeDtypeStruct((rows, group, width), jnp.bfloat16),
            jax.ShapeDtypeStruct((1, 1, MOST), jnp.float32),
        ),
        in_specs=[pl.BlockSpec(memory_space=pltpu.HBM), vmem],
        out_specs=(vmem, vmem),
        scratch_shapes=[
            pltpu.VMEM((2 * half - 1, rows, group, width), jnp.bfloat16),
            pltpu.VMEM((2, half, rows, group, width), jnp.bfloat16),
            pltpu.VMEM((width // LANE, rows * part_size, LANE), jnp.float32),
            *[pltpu.VMEM(message, jnp.bfloat16)] * 4,
            pltpu.VMEM((1, 128), jnp.float32),
            pltpu.VMEM((lines, 1, 128), jnp.float32),
            pltpu.VMEM((count, 1, 128), jnp.float32),
            pltpu.VMEM((width // 2 // LANE, part_size * 2 * rows, LANE), jnp.float32),
            pltpu.VMEM((count * rows, width), jnp.bfloat16),
            *[pltpu.VMEM(matrix, jnp.bfloat16)] * 6,
            pltpu.VMEM((count * rows, width), jnp.bfloat16),
            pltpu.VMEM((1, 128), jnp.float32),
            pltpu.SemaphoreType.DMA((2 * half - 1,)),
            pltpu.SemaphoreType.DMA((2, half, SUBS)),
            pltpu.SemaphoreType.DMA((2, half, SUBS)),
            pltpu.SemaphoreType.DMA((4,)),
            pltpu.SemaphoreType.DMA,
            pltpu.SemaphoreType.DMA((PARTS,)),
            pltpu.SemaphoreType.DMA,
            pltpu.SemaphoreType.DMA,
            pltpu.SemaphoreType.REGULAR,
        ],
        compiler_params=pltpu.CompilerParams(
            collective_id=0, has_side_effects=True, vmem_limit_bytes=53 * 2**20
        ),
    )(gradients, owners)


def solution(mesh):
    placed = (P("dp", "fsdp", None, None), P("dp", None))
    return jax.shard_map(
        on_device,
        mesh=mesh,
        in_specs=placed,
        out_specs=(P("fsdp", "dp", None), P("dp", "fsdp", None)),
        check_vma=False,
    )
```

time: 290 us -> 84.6 us (0.29)
  blocking collectives: 166 us -> 0 us
  Pallas kernels: 0 us -> 81.8 us
  waiting for transfers between devices: 64.4 us -> 0 us
  between operations: 16.9 us -> 0.65 us
  matrix products: 15.2 us -> 0 us
  local copies, waits for them, and re-layouts: 13.9 us -> 1.95 us
  starting transfers between devices: 6.51 us -> 0 us
  other arithmetic: 4.46 us -> 0 us
    unnamed x1 -> x0, blocking collectives: 128 us -> none
    pallas_call x0 -> x1, Pallas kernels: none -> 81.8 us  [on_device(): pl.pallas_call(functools.partial(step_kernel, planes, count), out_shape=(...]
    reduce_scatter x1 -> x0, waiting for transfers between devices: 64.4 us -> none  [on_device(): lax.psum_scatter(gradients[0].astype(jnp.float32).astype(jnp.bfloat16), '...]
    all_to_all x1 -> x0, blocking collectives: 38.1 us -> none  [on_device(): lax.all_to_all(summed, 'fsdp', split_axis=1, concat_axis=0, tiled=True)]
    dot_general x9 -> x0, matrix products: 15.2 us -> none  [product(): return jnp.dot(left_side, right_side, preferred_element_type=jnp.float32)]
    unnamed x14 -> x4, local copies, waits for them, and re-layouts: 12.8 us -> 1.95 us
    all_to_all x1 -> x0, starting transfers between devices: 6.47 us -> none  [on_device(): lax.all_to_all(block_update[:, None, :], 'fsdp', split_axis=0, concat_axi...]
  transfers between devices with their start and end apart: 2 -> 0, of which waited for: 1 -> 0; matrix products, arithmetic and copies ran while one was open for 1% -> 0% of each run, Pallas kernels for 0% -> 0%
where the time goes in v1:
time: 84.6 us; the launch traced here: 84.4 us
  Pallas kernels  81.8 us (97%)
  local copies, waits for them, and re-layouts  1.95 us (2%)
    pallas_call x1, Pallas kernels, on_device(): pl.pallas_call(functools.partial(step_kernel, planes, count), out_shape=(...  81.8 us
    unnamed x4, local copies, waits for them, and re-layouts  1.95 us

profile of v1, /device:TPU:1, one launch (start us, length us, event | category | flops | bytes accessed | tf_op | source)
XLA Modules:
  0.0 84.4 jit_solution(9621057988026282715)
XLA Ops:
  0.6 0.0 copy-start
  0.6 0.6 copy-done
  1.3 81.8 %shard_map.41 = (bf16[8,64,512]{2,1,0:T(8,128)(2,1)S(1)}, f32[1,1,2]{2,1,0:T(1,128)S(1)}) custom-call(bf16[1,8,512,512]{3,2,1,0:T(8,128)(2,1)} %x_ref.1, s32[1,64]{1,0:T(1,128)S(1)} %copy-done), custom_call_target="tpu_custom_call" | custom-call | tf_op jit(solution)/shard_map/pallas_call | solution.py:429
  83.1 0.8 copy.6
  83.9 0.5 copy.7
Async XLA Ops:
  0.6 0.7 copy-start

commit v2 on v1

--- a/solution.py
+++ b/solution.py
@@ -53,7 +53,7 @@
         odd = 1 - even if offset % 2 else even
         for pair in (first, 1 - first):
             column = 2 * pair + odd
-            send(row * (ACROSS // 2) + pair, (row * ACROSS + column) * CORES + core)
+            send(row * (ACROSS // 2) + pair, (row * ACROSS + column) * CORES + core, offset == 0)
 
 
 def blocks_stepped(index):
@@ -197,12 +197,16 @@
                 )
 
     def hand_out(part, batch):
-        def send(place, other):
+        def send(place, other, own_row):
             source = ready.at[part * part_size + place]
 
-            @pl.when(other != me)
-            def _():
+            def over():
                 push(source, gathered.at[me], other, push_sem.at[0], block_sem)
+
+            if not own_row:
+                over()
+                return
+            pl.when(other != me)(over)
 
             @pl.when(other == me)
             def _():
@@ -268,21 +272,15 @@
         pltpu.make_async_copy(back.at[me], returned.at[my_block], row_sem.at[my_wave]).start()
 
     def give_rows(quarter):
-        def to_lane(step, carry):
+        for step in range(quarter * lanes // 4, (quarter + 1) * lanes // 4):
             lane = within(my_lane + step, lanes)
             for offset in FAR_FIRST:
-                other = within(my_line + offset % lines, lines) * lanes + lane
-
-                @pl.when(other != me)
-                def _():
+                if step or offset:
+                    other = within(my_line + offset % lines, lines) * lanes + lane
                     push(
                         back.at[other], returned.at[my_block], other,
                         push_sem.at[1], row_sem.at[my_wave],
                     )
-
-            return carry
-
-        lax.fori_loop(quarter * lanes // 4, (quarter + 1) * lanes // 4, to_lane, 0)
 
     def first_rows():
         give_scale()

time: 84.6 us -> 84.7 us (level)
  no operation moved by 1% of the time
where the time goes in v2:
time: 84.7 us; the launch traced here: 84.6 us
  Pallas kernels  82 us (97%)
  local copies, waits for them, and re-layouts  1.95 us (2%)
    pallas_call x1, Pallas kernels, on_device(): pl.pallas_call(functools.partial(step_kernel, planes, count), out_shape=(...  82 us
    unnamed x4, local copies, waits for them, and re-layouts  1.95 us

profile of v2, /device:TPU:1, one launch (start us, length us, event | category | flops | bytes accessed | tf_op | source)
XLA Modules:
  0.0 84.6 jit_solution(17174693554577310728)
XLA Ops:
  0.6 0.0 copy-start
  0.6 0.6 copy-done
  1.3 82.0 %shard_map.41 = (bf16[8,64,512]{2,1,0:T(8,128)(2,1)S(1)}, f32[1,1,2]{2,1,0:T(1,128)S(1)}) custom-call(bf16[1,8,512,512]{3,2,1,0:T(8,128)(2,1)} %x_ref.1, s32[1,64]{1,0:T(1,128)S(1)} %copy-done), custom_call_target="tpu_custom_call" | custom-call | tf_op jit(solution)/shard_map/pallas_call | solution.py:427
  83.2 0.8 copy.6
  84.0 0.5 copy.7
Async XLA Ops:
  0.6 0.7 copy-start

commit v3 on v2

--- a/solution.py
+++ b/solution.py
@@ -11,8 +11,7 @@
 PARTS = 4
 SUBS = 2 * PARTS
 SLOTS = 4
-STARTS = (8, 12, 12, 12)
-PERIODS = 16
+PERIODS = 12
 LANE = 128
 LINES = 8
 FAR_FIRST = (4, -3, 3, -2, 2, -1, 1, 0)
@@ -327,10 +326,6 @@
         each.wait()
     first_relay(0)
     pl.semaphore_wait(plane_sem, lanes - 1)
-    begin = STARTS[-1]
-    for wave in reversed(range(PARTS - 1)):
-        begin = jnp.where(my_wave == wave, STARTS[wave], begin)
-
     def period(now, carry):
         for turn in range(SLOTS):
             far = SLOTS - 1 - turn
@@ -351,16 +346,17 @@
             lag = 2 * (half - 2) + (0 if turn == SLOTS - 1 else 1)
             last = now - lag
 
-            @pl.when((last >= 0) & (last < SUBS) & (lax.rem(last + SUBS, 2) == 1))
+            @pl.when((last >= 0) & (last < SUBS - 1) & (lax.rem(last + SUBS, 2) == 1))
             def _():
                 hand_out(lax.div(last, 2), (turn + 1) % SLOTS)
 
-            for number, stage in enumerate(stages):
-                if (number + SLOTS - 1) % SLOTS == turn:
-                    pl.when(now == begin + (number + SLOTS - 1) // SLOTS)(stage)
         return carry
 
     lax.fori_loop(0, PERIODS, period, 0)
+    for batch in range(SLOTS):
+        hand_out(PARTS - 1, batch)
+    for stage in stages:
+        stage()
 
     settle(column_scales, column_sem)
     mine_there = scales.at[pl.ds(my_lane * lines, lines)]

time: 84.7 us -> 81.8 us (0.966)
  Pallas kernels: 82 us -> 79.1 us
    pallas_call x1, Pallas kernels: 82 us -> 79.1 us  [on_device(): pl.pallas_call(functools.partial(step_kernel, planes, count), out_shape=(...]
where the time goes in v3:
time: 81.8 us; the launch traced here: 81.7 us
  Pallas kernels  79.1 us (97%)
  local copies, waits for them, and re-layouts  1.95 us (2%)
    pallas_call x1, Pallas kernels, on_device(): pl.pallas_call(functools.partial(step_kernel, planes, count), out_shape=(...  79.1 us
    unnamed x4, local copies, waits for them, and re-layouts  1.95 us

profile of v3, /device:TPU:1, one launch (start us, length us, event | category | flops | bytes accessed | tf_op | source)
XLA Modules:
  0.0 81.7 jit_solution(15615676230623010346)
XLA Ops:
  0.6 0.0 copy-start
  0.6 0.6 copy-done
  1.3 79.1 %shard_map.41 = (bf16[8,64,512]{2,1,0:T(8,128)(2,1)S(1)}, f32[1,1,2]{2,1,0:T(1,128)S(1)}) custom-call(bf16[1,8,512,512]{3,2,1,0:T(8,128)(2,1)} %x_ref.1, s32[1,64]{1,0:T(1,128)S(1)} %copy-done), custom_call_target="tpu_custom_call" | custom-call | tf_op jit(solution)/shard_map/pallas_call | solution.py:423
  80.4 0.8 copy.6
  81.2 0.5 copy.7
Async XLA Ops:
  0.6 0.7 copy-start

commit v4 on v3

--- a/solution.py
+++ b/solution.py
@@ -11,7 +11,7 @@
 PARTS = 4
 SUBS = 2 * PARTS
 SLOTS = 4
-PERIODS = 12
+PERIODS = 11
 LANE = 128
 LINES = 8
 FAR_FIRST = (4, -3, 3, -2, 2, -1, 1, 0)
@@ -330,7 +330,7 @@
         for turn in range(SLOTS):
             far = SLOTS - 1 - turn
             if far < half:
-                lag = 2 * (half - far) - 3 if far else 2 * (half - 2)
+                lag = -1 if far == half - 1 else half - 1 - far
                 sub = now - lag
 
                 @pl.when((sub >= 0) & (sub < SUBS))
@@ -343,7 +343,7 @@
                     else:
                         finish(sub)
 
-            lag = 2 * (half - 2) + (0 if turn == SLOTS - 1 else 1)
+            lag = half - 1 + (0 if turn == SLOTS - 1 else 1)
             last = now - lag
 
             @pl.when((last >= 0) & (last < SUBS - 1) & (lax.rem(last + SUBS, 2) == 1))

time: 81.8 us -> 80.8 us (0.988)
  Pallas kernels: 79.1 us -> 78.1 us
    pallas_call x1, Pallas kernels: 79.1 us -> 78.1 us  [on_device(): pl.pallas_call(functools.partial(step_kernel, planes, count), out_shape=(...]
where the time goes in v4:
time: 80.8 us; the launch traced here: 80.7 us
  Pallas kernels  78.1 us (97%)
  local copies, waits for them, and re-layouts  1.95 us (2%)
    pallas_call x1, Pallas kernels, on_device(): pl.pallas_call(functools.partial(step_kernel, planes, count), out_shape=(...  78.1 us
    unnamed x4, local copies, waits for them, and re-layouts  1.95 us

profile of v4, /device:TPU:1, one launch (start us, length us, event | category | flops | bytes accessed | tf_op | source)
XLA Modules:
  0.0 80.7 jit_solution(13389043045096321469)
XLA Ops:
  0.6 0.0 copy-start
  0.6 0.6 copy-done
  1.3 78.1 %shard_map.41 = (bf16[8,64,512]{2,1,0:T(8,128)(2,1)S(1)}, f32[1,1,2]{2,1,0:T(1,128)S(1)}) custom-call(bf16[1,8,512,512]{3,2,1,0:T(8,128)(2,1)} %x_ref.1, s32[1,64]{1,0:T(1,128)S(1)} %copy-done), custom_call_target="tpu_custom_call" | custom-call | tf_op jit(solution)/shard_map/pallas_call | solution.py:423
  79.4 0.8 copy.6
  80.2 0.5 copy.7
Async XLA Ops:
  0.6 0.7 copy-start
